TPU v7x, 512 devices: a whole 4x8x8 slice. The times are simulated.
512 devices in a mesh: row: 32 (over z_lo, y), col: 16 (over z_hi, x, core).
Axes of the slice: x: 4, y: 8, z: 8 (z_hi: 2, z_lo: 4; z = z_hi * 4 + z_lo), core: 2. Of those that a mesh axis runs over, the one named last changes fastest.
Arguments:
- center: bfloat16 [2048, 8192], P('col', 'row'), may hold values from -6 to 6
- radius: bfloat16 [2048, 8192], P('col', 'row'), may hold values from 0.049804688 to 1
- grad_center: bfloat16 [2048, 8192], P('row', 'col'), may hold values from -6 to 6
- grad_radius: bfloat16 [2048, 8192], P('row', 'col'), may hold values from -6 to 6
- weight: bfloat16 [8192, 8192], P('row', 'col'), may hold values from -0.0625 to 0.0625
- active: int32 [2048, 8192], P('col', 'row'), may hold values 0 or 1
Outputs:
- center_in: float32 [2048, 8192], P('col', 'row')
- radius_in: float32 [2048, 8192], P('col', 'row')
- weight_grad: float32 [8192, 8192], P('row', 'col')
All inputs are finite; a program needn't handle non-finite values. No bound on the sum of `active` on one device may be relied on, other than what follows from the above.
Results may differ from a plain program's by a relative error of at most 0.0003.
Values may be sent and summed in bfloat16 or wider, within the bound.
A program may use at most 64 MiB of HBM per device.

v0:
```python
import jax
import jax.numpy as jnp
from jax import lax
from jax.sharding import PartitionSpec as P


def on_device(center, radius, grad_center, grad_radius, weight, active):
    magnitude = jnp.abs(weight)
    stacked = jnp.stack((grad_center, grad_radius))
    inputs = lax.all_gather(jnp.stack((center, radius)), "col", axis=1, tiled=True)
    contract_out = (((1,), (1,)), ((), ()))
    contract_tok = (((0,), (0,)), ((), ()))
    total_tokens = inputs.shape[1]
    panels = lax.all_gather(stacked, "row", axis=1, tiled=True)
    through_center = lax.dot_general(
        panels[0], weight, contract_out, preferred_element_type=jnp.float32
    )
    through_radius = lax.dot_general(
        panels[1], magnitude, contract_out, preferred_element_type=jnp.float32
    )
    partial_terms = jnp.stack((through_center, through_radius))
    center_acc = lax.dot_general(
        inputs[0], panels[0], contract_tok, preferred_element_type=jnp.float32
    )
    radius_acc = lax.dot_general(
        inputs[1], panels[1], contract_tok, preferred_element_type=jnp.float32
    )
    center_acc, radius_acc = (center_acc, radius_acc)
    summed = lax.psum_scatter(partial_terms, "col", scatter_dimension=1, tiled=True)
    gating = active.astype(jnp.float32)
    center_in = gating * summed[0]
    radius_in = gating * summed[1]
    scale_factor = jnp.float32(1.0) / jnp.sqrt(jnp.float32(total_tokens))
    weight_grad = (center_acc + jnp.sign(weight).astype(jnp.float32) * radius_acc) * scale_factor
    return (center_in, radius_in, weight_grad)


def solution(mesh):
    in_specs = (
        P("col", "row"),
        P("col", "row"),
        P("row", "col"),
        P("row", "col"),
        P("row", "col"),
        P("col", "row"),
    )
    out_specs = (P("col", "row"), P("col", "row"), P("row", "col"))
    return jax.shard_map(
        on_device, mesh=mesh, in_specs=in_specs, out_specs=out_specs, check_vma=False
    )
```

profile of v0, /device:TPU:8, one launch (start us, length us, event | category | flops | bytes accessed | tf_op | source)
XLA Modules:
  0.0 365.3 jit_solution(8215343059179930053)
XLA Ops:
  7.2 0.0 all-gather.3.cloned.1.call-start
  7.2 1.5 pad_maximum_fusion.1
  8.8 0.0 all-gather.3.cloned.1.call-update
  8.8 0.0 all-gather.5.cloned.1.call-start
  8.8 1.5 pad_maximum_fusion.2
  10.4 0.0 all-gather.5.cloned.1.call-update
  10.4 0.0 copy-start.1
  10.4 0.0 reduce-scatter.2.cloned.1.call-start
  10.5 163.6 %all-gather.3.cloned.1.call-done = bf16[2,2048,512]{2,1,0:T(8,128)(2,1)} async-done(((bf16[2,64,512]{2,1,0:T(8,128)(2,1)}), bf16[2,2048,512]{2,1,0:T(8,128)(2,1)}) %all-gather.3.cloned.1.call-update) | async-done | bytes 4194320 | tf_op jit(solution)/shard_map/all_gather | solution.py:14
  174.1 0.0 copy-start
  174.1 2.5 convolution_bitcast_fusion.1
  176.6 0.0 copy-done.1
  176.6 0.4 copy-done
  177.0 0.7 convolution_bitcast_fusion
  177.7 2.2 pad_maximum_fusion
  180.0 0.0 reduce-scatter.2.cloned.1.call-update
  180.0 62.9 %all-gather.5.cloned.1.call-done = bf16[2,2048,256]{2,1,0:T(8,128)(2,1)} async-done(((bf16[2,128,256]{2,1,0:T(8,128)(2,1)}), bf16[2,2048,256]{2,1,0:T(8,128)(2,1)}) %all-gather.5.cloned.1.call-update) | async-done | bytes 2097168 | tf_op jit(solution)/shard_map/all_gather | solution.py:10
  242.9 0.0 copy-start.3
  242.9 2.8 fusion
  245.7 0.0 copy-done.3
  245.7 0.0 copy-start.2
  245.7 3.2 fusion.4
  248.9 108.1 %reduce-scatter.2.cloned.1.call-done = f32[2,128,256]{2,1,0:T(8,128)} async-done(((f32[2,2048,256]{2,1,0:T(8,128)}), f32[2,128,256]{2,1,0:T(8,128)}) %reduce-scatter.2.cloned.1.call-update) | async-done | bytes 262160 | tf_op jit(solution)/shard_map/reduce_scatter | solution.py:29
  357.1 0.0 copy-done.2
  357.1 1.7 fusion.6
Async XLA Ops:
  7.2 166.9 %all-gather.3.cloned.1.call-start = ((), (), s32[]{:S(2)}) async-start(), calls=%async_computation.1 | async-start | bytes 4325376 | tf_op jit(solution)/shard_map/all_gather | solution.py:14
  8.8 234.1 %all-gather.5.cloned.1.call-start = ((), (), s32[]{:S(2)}) async-start(), calls=%async_computation.3 | async-start | bytes 2228224 | tf_op jit(solution)/shard_map/all_gather | solution.py:10
  10.4 166.2 %copy-start.1 = (bf16[256,512]{1,0:T(8,128)(2,1)S(1)}, bf16[256,512]{1,0:T(8,128)(2,1)}, u32[]{:S(2)}) copy-start(bf16[256,512]{1,0:T(8,128)(2,1)} %param.10) | copy-start | bytes 786436
  10.4 346.6 %reduce-scatter.2.cloned.1.call-start = ((), (), s32[]{:S(2)}) async-start(), calls=%async_computation.2 | async-start | bytes 4456448 | tf_op jit(solution)/shard_map/reduce_scatter | solution.py:29
  174.1 2.9 copy-start
  242.9 2.8 copy-start.3
  245.7 111.3 %copy-start.2 = (s32[128,256]{1,0:T(8,128)S(1)}, s32[128,256]{1,0:T(8,128)}, u32[]{:S(2)}) copy-start(s32[128,256]{1,0:T(8,128)} %param.11) | copy-start | bytes 393220
Sparse Core Ops, SparseCore 0:
  10.7 163.3 all-gather.2
  178.0 64.8 all-gather.4
  247.8 109.1 reduce-scatter.1
where the time goes:
time: 366 us; the launch traced here: 365 us
  waiting for transfers between devices  335 us (92%)
  between operations  13.8 us (4%)
  matrix products  9.2 us (3%)
  other arithmetic  7.01 us (2%)
    all_gather x1, waiting for transfers between devices, on_device(): panels = lax.all_gather(stacked, 'row', axis=1, tiled=True)  164 us
    reduce_scatter x1, waiting for transfers between devices, on_device(): lax.psum_scatter(partial_terms, 'col', scatter_dimension=1, tiled=True)  108 us
    all_gather x1, waiting for transfers between devices, on_device(): lax.all_gather(jnp.stack((center, radius)), 'col', axis=1, tiled=True)  62.9 us
  transfers between devices with their start and end apart: 3, of which 3 were waited for; matrix products, arithmetic and copies ran while one was open for 4% of the time, Pallas kernels for 0%

commit v1 on v0

--- a/solution.py
+++ b/solution.py
@@ -11,7 +11,9 @@
     contract_out = (((1,), (1,)), ((), ()))
     contract_tok = (((0,), (0,)), ((), ()))
     total_tokens = inputs.shape[1]
-    panels = lax.all_gather(stacked, "row", axis=1, tiled=True)
+    panels = jnp.concatenate(
+        lax.all_to_all(jnp.stack([stacked] * lax.axis_size("row")), "row", 0, 0), axis=1
+    )
     through_center = lax.dot_general(
         panels[0], weight, contract_out, preferred_element_type=jnp.float32
     )

time: 366 us -> 285 us (0.78)
  waiting for transfers between devices: 335 us -> 241 us
  starting transfers between devices: 0.12 us -> 13.4 us
  local copies, waits for them, and re-layouts: 0.41 us -> 5.62 us
    all_gather x1 -> x0, waiting for transfers between devices: 164 us -> none  [on_device(): panels = lax.all_gather(stacked, 'row', axis=1, tiled=True)]
    all_to_all x0 -> x1, waiting for transfers between devices: none -> 101 us  [on_device(): lax.all_to_all(jnp.stack([stacked] * lax.axis_size('row')), 'row', 0, 0)]
    all_gather x1, waiting for transfers between devices: 62.9 us -> 26.5 us  [on_device(): lax.all_gather(jnp.stack((center, radius)), 'col', axis=1, tiled=True)]
    all_to_all x0 -> x1, starting transfers between devices: none -> 13.3 us  [on_device(): lax.all_to_all(jnp.stack([stacked] * lax.axis_size('row')), 'row', 0, 0)]
    reduce_scatter x1, waiting for transfers between devices: 108 us -> 113 us  [on_device(): lax.psum_scatter(partial_terms, 'col', scatter_dimension=1, tiled=True)]
where the time goes in v1:
time: 285 us
  waiting for transfers between devices  241 us (85%)
  between operations  14.1 us (5%)
  starting transfers between devices  13.4 us (5%)
  matrix products  5.83 us (2%)
  local copies, waits for them, and re-layouts  5.62 us (2%)
  other arithmetic  5.46 us (2%)
    reduce_scatter x1, waiting for transfers between devices, on_device(): lax.psum_scatter(partial_terms, 'col', scatter_dimension=1, tiled=True)  113 us
    all_to_all x1, waiting for transfers between devices, on_device(): lax.all_to_all(jnp.stack([stacked] * lax.axis_size('row')), 'row', 0, 0)  101 us
    all_gather x1, waiting for transfers between devices, on_device(): lax.all_gather(jnp.stack((center, radius)), 'col', axis=1, tiled=True)  26.5 us
    all_to_all x1, starting transfers between devices, on_device(): lax.all_to_all(jnp.stack([stacked] * lax.axis_size('row')), 'row', 0, 0)  13.3 us
  transfers between devices with their start and end apart: 3, of which 3 were waited for; matrix products, arithmetic and copies ran while one was open for 4% of the time, Pallas kernels for 0%

profile of v1, /device:TPU:8, one launch (start us, length us, event | category | flops | bytes accessed | tf_op | source)
XLA Modules:
  0.0 285.0 jit_solution(14643400405816463906)
XLA Ops:
  7.2 0.9 pad_maximum_fusion.1
  8.1 2.5 stack.23
  10.5 0.0 copy-start.3
  10.5 0.0 copy-start.4
  10.5 13.3 %all-to-all-start = ((bf16[32,2,64,512]{3,2,1,0:T(8,128)(2,1)}), bf16[32,2,64,512]{3,2,1,0:T(8,128)(2,1)}, u32[]{:S(2)}, u32[]{:S(2)}) async-start(bf16[32,2,64,512]{3,2,1,0:T(8,128)(2,1)} %stack.23), calls=%async_computation | async-start | bytes 8388608 | tf_op jit(solution)/shard_map/all_to_all | solution.py:15
  23.9 0.0 all-gather.2.cloned.1.call-start
  23.9 0.0 copy-done.3
  23.9 0.0 copy-done.4
  23.9 0.7 pad_maximum_fusion.2
  24.6 0.0 all-gather.2.cloned.1.call-update
  24.6 0.0 reduce-scatter.2.cloned.1.call-start
  24.7 100.6 %all-to-all-done = bf16[32,2,64,512]{3,2,1,0:T(8,128)(2,1)} async-done(((bf16[32,2,64,512]{3,2,1,0:T(8,128)(2,1)}), bf16[32,2,64,512]{3,2,1,0:T(8,128)(2,1)}, u32[]{:S(2)}, u32[]{:S(2)}) %all-to-all-start) | async-done | bytes 4194336 | tf_op jit(solution)/shard_map/all_to_all | solution.py:15
  125.3 0.0 copy-start.1
  125.3 2.6 fusion.6
  127.9 0.0 copy-start
  127.9 0.0 copy-done.1
  127.9 0.7 convolution_bitcast_fusion.1
  128.6 0.6 copy-done
  129.2 0.7 convolution_bitcast_fusion
  129.9 2.2 pad_maximum_fusion
  132.2 0.0 reduce-scatter.2.cloned.1.call-update
  132.2 26.5 %all-gather.2.cloned.1.call-done = bf16[2,2048,256]{2,1,0:T(8,128)(2,1)} async-done(((bf16[2,128,256]{2,1,0:T(8,128)(2,1)}), bf16[2,2048,256]{2,1,0:T(8,128)(2,1)}) %all-gather.2.cloned.1.call-update) | async-done | bytes 2097168 | tf_op jit(solution)/shard_map/all_gather | solution.py:10
  158.6 0.0 copy-start.5
  158.6 2.8 fusion.2
  161.4 0.0 copy-done.5
  161.4 0.0 copy-start.2
  161.5 1.6 fusion.1
  163.0 113.4 %reduce-scatter.2.cloned.1.call-done = f32[2,128,256]{2,1,0:T(8,128)} async-done(((f32[2,2048,256]{2,1,0:T(8,128)}), f32[2,128,256]{2,1,0:T(8,128)}) %reduce-scatter.2.cloned.1.call-update) | async-done | bytes 262160 | tf_op jit(solution)/shard_map/reduce_scatter | solution.py:31
  276.4 0.0 copy-done.2
  276.4 1.7 fusion.4
Async XLA Ops:
  10.5 13.4 %copy-start.3 = (bf16[128,256]{1,0:T(8,128)(2,1)S(1)}, bf16[128,256]{1,0:T(8,128)(2,1)}, u32[]{:S(2)}) copy-start(bf16[128,256]{1,0:T(8,128)(2,1)} %param.7) | copy-start | bytes 196612
  10.5 13.4 %copy-start.4 = (bf16[128,256]{1,0:T(8,128)(2,1)S(1)}, bf16[128,256]{1,0:T(8,128)(2,1)}, u32[]{:S(2)}) copy-start(bf16[128,256]{1,0:T(8,128)(2,1)} %param.6) | copy-start | bytes 196612
  10.5 114.8 %all-to-all-start = ((bf16[32,2,64,512]{3,2,1,0:T(8,128)(2,1)}), bf16[32,2,64,512]{3,2,1,0:T(8,128)(2,1)}, u32[]{:S(2)}, u32[]{:S(2)}) async-start(bf16[32,2,64,512]{3,2,1,0:T(8,128)(2,1)} %stack.23), calls=%async_computation | async-start | bytes 8388608 | tf_op jit(solution)/shard_map/all_to_all | solution.py:15
  23.9 134.8 %all-gather.2.cloned.1.call-start = ((), (), s32[]{:S(2)}) async-start(), calls=%async_computation.3 | async-start | bytes 2228224 | tf_op jit(solution)/shard_map/all_gather | solution.py:10
  24.6 251.8 %reduce-scatter.2.cloned.1.call-start = ((), (), s32[]{:S(2)}) async-start(), calls=%async_computation.2 | async-start | bytes 4456448 | tf_op jit(solution)/shard_map/reduce_scatter | solution.py:31
  125.3 2.6 copy-start.1
  127.9 1.3 copy-start
  158.6 2.8 copy-start.5
  161.4 115.0 %copy-start.2 = (s32[128,256]{1,0:T(8,128)S(1)}, s32[128,256]{1,0:T(8,128)}, u32[]{:S(2)}) copy-start(s32[128,256]{1,0:T(8,128)} %param.11) | copy-start | bytes 393220
Sparse Core Ops, SparseCore 0:
  28.6 129.9 all-gather.1
  163.6 112.8 reduce-scatter.1
